TPU v7x, 512 devices: a whole 4x4x16 slice. The times are simulated.
512 devices in a mesh: dp: 32 (over z, y_hi), tm: 4 (over y_lo, core), mp: 4 (over x).
Axes of the slice: x: 4, y: 4 (y_hi: 2, y_lo: 2; y = y_hi * 2 + y_lo), z: 16, core: 2. Of those that a mesh axis runs over, the one named last changes fastest.
Arguments:
- activations: bfloat16 [32, 8, 5, 40, 1280], P('dp', 'tm', None, None, 'mp'), may hold values from -1200 to 1200
- norm_gain: float32 [1280], P('mp'), may hold values from 0.25 to 1.75
- norm_bias: float32 [1280], P('mp'), may hold values from -3 to 3
- spatial_weight: bfloat16 [9, 1280, 1280], P(None, 'mp', 'tm'), may hold values from -0.0546875 to 0.0546875
- temporal_weight: bfloat16 [3, 1280, 1280], P(None, 'tm', 'mp'), may hold values from -0.09375 to 0.09375
- cotangent: bfloat16 [32, 8, 5, 40, 1280], P('dp', 'tm', None, None, 'mp'), may hold values from -6 to 6
Outputs:
- block_output: bfloat16 [32, 8, 5, 40, 1280], P('dp', 'tm', None, None, 'mp')
- temporal_grad: float32 [3, 1280, 1280], P(None, 'tm', 'mp')
All inputs are finite; a program needn't handle non-finite values.
Results may differ from a plain program's by a relative error of at most 0.0058.
Values may be sent and summed in bfloat16 or wider, within the bound.
A program may use at most 64 MiB of HBM per device.

v0:
```python
import jax
import jax.numpy as jnp
from jax import lax
from jax.sharding import PartitionSpec as P

CHANNELS = 1280
GROUPS = 32


epsilon = 1e-05


def clip_gather(block):
    return lax.all_gather(block, "tm", axis=1, tiled=True)


def group_mean(channel_sums, total_count, group_width):
    grouped = channel_sums.reshape(-1, group_width).sum(axis=1) / total_count
    return jnp.repeat(grouped, group_width)


def body(activations, norm_gain, norm_bias, spatial_weight, temporal_weight, cotangent):
    frames_dev = activations.shape[1]
    rows_band = activations.shape[2]
    columns = activations.shape[3]
    width_mp = activations.shape[4]
    width_tm = spatial_weight.shape[2]
    tm_count = lax.axis_size("tm")
    mp_count = lax.axis_size("mp")
    frames_all = frames_dev * tm_count
    group_width = CHANNELS // GROUPS
    total_count = float(frames_all * rows_band * columns * group_width)
    values = clip_gather(activations).astype(jnp.float32)
    mean_full = group_mean(values.sum(axis=(0, 1, 2, 3)), total_count, group_width)
    centered = values - mean_full
    var_full = group_mean((centered * centered).sum(axis=(0, 1, 2, 3)), total_count, group_width)
    normed = centered * lax.rsqrt(var_full + epsilon) * norm_gain + norm_bias
    hidden = jax.nn.silu(normed).astype(jnp.bfloat16)
    padded = jnp.pad(hidden[0], ((0, 0), (1, 1), (1, 1), (0, 0)))
    portion = padded
    summed = jnp.zeros(
        (lax.axis_size("mp") * (frames_all // mp_count) * rows_band * columns, width_tm),
        jnp.float32,
    )
    for spatial_tap_index in range(9):
        row_shift = spatial_tap_index // 3
        col_shift = spatial_tap_index % 3
        spatial_window = portion[
            :, row_shift : row_shift + rows_band, col_shift : col_shift + columns, :
        ].reshape(-1, width_mp)
        summed = summed + jnp.dot(
            spatial_window, spatial_weight[spatial_tap_index], preferred_element_type=jnp.float32
        )
    spatial_out = lax.psum_scatter(
        summed.reshape(
            lax.axis_size("mp") * (frames_all // mp_count), rows_band, columns, width_tm
        ),
        "mp",
        scatter_dimension=0,
        tiled=True,
    ).astype(jnp.bfloat16)
    spatial_all = lax.all_gather(spatial_out, "mp", axis=0, tiled=True)
    spatial_pad = jnp.pad(spatial_all, ((1, 1), (0, 0), (0, 0), (0, 0)))
    portion = spatial_pad
    summed = jnp.zeros(
        (lax.axis_size("tm") * frames_dev * rows_band * columns, width_mp), jnp.float32
    )
    for temporal_tap_index in range(3):
        temporal_window = portion[
            temporal_tap_index : temporal_tap_index + lax.axis_size("tm") * frames_dev
        ].reshape(-1, width_tm)
        summed = summed + jnp.dot(
            temporal_window, temporal_weight[temporal_tap_index], preferred_element_type=jnp.float32
        )
    block_output = lax.psum_scatter(
        summed.reshape(lax.axis_size("tm") * frames_dev, rows_band, columns, width_mp),
        "tm",
        scatter_dimension=0,
        tiled=True,
    ).astype(jnp.bfloat16)[None]
    grad_all = clip_gather(cotangent)[0].reshape(-1, width_mp)
    tap_grads = []
    for tap_index in range(3):
        window = spatial_pad[tap_index : tap_index + frames_all].reshape(-1, width_tm)
        tap_grads.append(
            lax.dot_general(
                window, grad_all, (((0,), (0,)), ((), ())), preferred_element_type=jnp.float32
            )
        )
    clip_count = lax.axis_size("dp")
    temporal_grad = lax.psum(jnp.stack(tap_grads), "dp") / clip_count
    return (block_output, temporal_grad)


def solution(mesh):
    in_specs = (
        P("dp", "tm", None, None, "mp"),
        P("mp"),
        P("mp"),
        P(None, "mp", "tm"),
        P(None, "tm", "mp"),
        P("dp", "tm", None, None, "mp"),
    )
    out_specs = (P("dp", "tm", None, None, "mp"), P(None, "tm", "mp"))
    return jax.shard_map(body, mesh=mesh, in_specs=in_specs, out_specs=out_specs, check_vma=False)
```

profile of v0, /device:TPU:4, one launch (start us, length us, event | category | flops | bytes accessed | tf_op | source)
XLA Modules:
  0.0 457.6 jit_solution(11776561558499727205)
XLA Ops:
  7.2 11.3 %all_gather.9 = bf16[1,8,5,40,320]{4,3,2,0,1:T(8,128)(2,1)S(1)} all-gather(bf16[1,2,5,40,320]{4,3,2,0,1:T(8,128)(2,1)} %bitcast.101), channel_id=1, replica_groups=mesh['dp'=32,'tm'=4,'mp'=4] {'tm'}, dimensions={1}, use_global_device_ids=true | all-gather | bytes 1280000 | tf_op jit(solution)/shard_map/all_gather | solution.py:14
  20.0 0.9 fusion.55
  20.8 0.9 fusion.10
  21.7 2.9 pad_slice_fusion
  24.6 0.8 fusion.23
  25.4 0.8 convolution_add_fusion.9
  26.2 0.8 convolution_add_fusion.8
  27.1 0.8 convolution_add_fusion.7
  27.9 0.8 convolution_add_fusion.6
  28.7 0.8 convolution_add_fusion.5
  29.5 0.8 convolution_add_fusion.4
  30.3 0.8 convolution_add_fusion.3
  31.1 0.8 convolution_add_fusion.2
  31.9 2.1 copy.16
  34.1 0.9 copy-done.6
  35.0 11.1 %all_gather.11 = bf16[1,8,5,40,320]{4,3,2,0,1:T(8,128)(2,1)S(1)} all-gather(bf16[1,2,5,40,320]{4,3,2,0,1:T(8,128)(2,1)S(1)} %bitcast.102), channel_id=1, replica_groups=mesh['dp'=32,'tm'=4,'mp'=4] {'tm'}, dimensions={1}, use_global_device_ids=true | all-gather | bytes 1280000 | tf_op jit(solution)/shard_map/all_gather | solution.py:14
  46.1 31.0 %reduce-scatter.3.cloned.1.call-done = f32[2,5,40,320]{3,2,1,0:T(8,128)} async-done(((f32[8,5,40,320]{3,2,1,0:T(8,128)}), f32[2,5,40,320]{3,2,1,0:T(8,128)}) %reduce-scatter.3.cloned.1.call-update) | async-done | bytes 512016 | tf_op jit(solution)/shard_map/reduce_scatter | solution.py:54
  77.1 1.1 convert_element_type.18
  78.2 16.2 %all_gather.10 = bf16[8,5,40,320]{3,2,1,0:T(8,128)(2,1)S(1)} all-gather(bf16[2,5,40,320]{3,2,1,0:T(8,128)(2,1)S(1)} %convert_element_type.18), channel_id=1, replica_groups=mesh['dp'=32,'tm'=4,'mp'=4] {'mp'}, dimensions={0}, use_global_device_ids=true | all-gather | bytes 1280000 | tf_op jit(solution)/shard_map/all_gather | solution.py:62
  94.6 0.8 convolution_bitcast_fusion
  95.4 0.8 convolution_bitcast_fusion.2
  96.2 0.8 convolution_bitcast_fusion.1
  97.0 1.2 pad_maximum_fusion
  98.3 0.5 copy-done.1
  99.0 0.8 fusion.13
  99.8 0.8 convolution_add_fusion.1
  101.1 0.8 convolution_add_fusion
  101.9 2.1 copy.17
  104.1 309.0 %all-reduce.4.cloned.1.call-done = f32[3,320,320]{2,1,0:T(8,128)} async-done(((f32[3,320,320]{2,1,0:T(8,128)}), f32[3,320,320]{2,1,0:T(8,128)}) %all-reduce.4.cloned.1.call-update) | async-done | bytes 1228816 | tf_op jit(solution)/shard_map/psum | solution.py:91
  413.0 2.6 broadcast_multiply_fusion
  415.6 33.6 %reduce-scatter.5.cloned.1.call-done = f32[2,5,40,320]{3,2,1,0:T(8,128)} async-done(((f32[8,5,40,320]{3,2,1,0:T(8,128)}), f32[2,5,40,320]{3,2,1,0:T(8,128)}) %reduce-scatter.5.cloned.1.call-update) | async-done | bytes 512016 | tf_op jit(solution)/shard_map/reduce_scatter | solution.py:75
  449.2 1.8 convert_bitcast_fusion
  (35 shorter events, 2.5 us)
Async XLA Ops:
  7.2 12.8 %copy-start.8 = (f32[320]{0:T(512)S(1)}, f32[320]{0:T(512)}, u32[]{:S(2)}) copy-start(f32[320]{0:T(512)} %param.7) | copy-start | bytes 3844
  7.2 12.8 %copy-start.7 = (f32[320]{0:T(512)S(1)}, f32[320]{0:T(512)}, u32[]{:S(2)}) copy-start(f32[320]{0:T(512)} %param.8) | copy-start | bytes 3844
  7.2 69.9 %reduce-scatter.3.cloned.1.call-start = ((), (), s32[]{:S(2)}) async-start(), calls=%async_computation.2 | async-start | bytes 3072000 | tf_op jit(solution)/shard_map/reduce_scatter | solution.py:54
  21.7 2.9 copy-start.4
  34.0 1.0 copy-start.6
  34.1 379.0 %all-reduce.4.cloned.1.call-start = ((), (), s32[]{:S(2)}) async-start(), calls=%async_computation.4 | async-start | bytes 2949120 | tf_op jit(solution)/shard_map/psum | solution.py:91
  94.6 1.6 copy-start
  94.6 1.6 copy-start.2
  97.0 1.8 copy-start.1
  97.0 2.0 copy-start.5
  98.3 351.0 %reduce-scatter.5.cloned.1.call-start = ((), (), s32[]{:S(2)}) async-start(), calls=%async_computation.3 | async-start | bytes 3072000 | tf_op jit(solution)/shard_map/reduce_scatter | solution.py:75
  99.8 1.3 copy-start.3
Sparse Core Ops, SparseCore 0:
  34.2 42.9 reduce-scatter.2
  98.4 314.6 all-reduce.3
  416.1 33.0 reduce-scatter.4
where the time goes:
time: 459 us; the launch traced here: 458 us
  waiting for transfers between devices  374 us (81%)
  blocking collectives  38.6 us (8%)
  between operations  14 us (3%)
  matrix products  12 us (3%)
  local copies, waits for them, and re-layouts  9.87 us (2%)
  other arithmetic  9.39 us (2%)
    psum x1, waiting for transfers between devices, body(): temporal_grad = lax.psum(jnp.stack(tap_grads), 'dp') / clip_count  309 us
    reduce_scatter x1, waiting for transfers between devices, body(): lax.psum_scatter(summed.reshape(lax.axis_size('tm') * frames_dev, rows_ba...  33.6 us
    reduce_scatter x1, waiting for transfers between devices, body(): lax.psum_scatter(summed.reshape(lax.axis_size('mp') * (frames_all // mp_c...  31 us
    all_gather x2, blocking collectives, clip_gather(): return lax.all_gather(block, 'tm', axis=1, tiled=True)  22.4 us
    all_gather x1, blocking collectives, body(): spatial_all = lax.all_gather(spatial_out, 'mp', axis=0, tiled=True)  16.2 us
  transfers between devices with their start and end apart: 3, of which 3 were waited for; matrix products, arithmetic and copies ran while one was open for 2% of the time, Pallas kernels for 0%

commit v1 on v0

v1 whole, which is shorter than its diff:
```python
import jax
import jax.numpy as jnp
from jax import lax
from jax.experimental import pallas as pl
from jax.experimental.pallas import tpu as pltpu
from jax.sharding import PartitionSpec as P

MESH = pl.DeviceIdType.MESH
F32, BF16 = jnp.float32, jnp.bfloat16

CH = 320
GROUP = 40
ROWS, COLS, PCOLS = 5, 40, 48
FR = ROWS * COLS
FP = 208
CUT = 112
HR = ROWS * PCOLS
CHUNK = 64
EPS = 1e-05


def dot(a, b, **kw):
    return jnp.dot(a, b, preferred_element_type=F32, **kw)


def kernel(
    act, gain, bias, ws, wt, cot, out, gout,
    actv, cotv, wsv, wtv, stats, hid, cotp, part, far_r, far_l, near, spat,
    grad, s1r, s2r, s1l, s2l, r1r, r2r, r1l, r2l, yhs, yhr, gath,
    tpre, tsame, tsend0, tsend1, ysend, yrecv, lsem, ssem, rsem,
):
    dp, tm, mp = lax.axis_index("dp"), lax.axis_index("tm"), lax.axis_index("mp")
    core, yl = lax.rem(tm, 2), lax.div(tm, 2)
    z, yh = lax.div(dp, 2), lax.rem(dp, 2)
    tc = tm + 1 - 2 * core
    ty = lax.rem(tm + 2, 4)
    tyc = lax.rem(tc + 2, 4)

    def zdev(s):
        return {"dp": lax.rem(dp + (2 * s + 32), 32)}

    def xdev(s):
        return {"mp": lax.rem(mp + (s + 4), 4)}

    names = {}

    def rc(name, src, dst, dev):
        i = names.setdefault(name, len(names))
        return pltpu.make_async_remote_copy(
            src_ref=src, dst_ref=dst, send_sem=ssem.at[i], recv_sem=rsem.at[i],
            device_id=dev, device_id_type=MESH,
        )

    started = []

    def send(name, src, dst, dev):
        c = rc(name, src, dst, dev)
        c.start()
        started.append(c)

    def arrived(name, dst, dev):
        rc(name, dst, dst, dev).wait_recv()

    c_act = pltpu.make_async_copy(act, actv, lsem.at[0])
    c_ws = pltpu.make_async_copy(ws, wsv, lsem.at[1])
    c_cot = pltpu.make_async_copy(cot, cotv, lsem.at[2])
    c_wt = pltpu.make_async_copy(wt, wtv, lsem.at[3])
    for c in (c_act, c_ws, c_cot, c_wt):
        c.start()
    yhd = {"dp": dp + 1 - 2 * yh}
    peers = [{"tm": tc}, {"tm": ty}, {"tm": tyc}, xdev(1), xdev(-1)]
    peers += [zdev(1), zdev(-1), zdev(2), zdev(-2), yhd]
    barrier = pltpu.get_barrier_semaphore()
    for p in peers:
        pl.semaphore_signal(barrier, inc=1, device_id=p, device_id_type=MESH)

    zrows = jnp.zeros((8, PCOLS, CH), BF16)
    hid[:, pl.ds(0, PCOLS), :] = zrows
    hid[:, pl.ds(PCOLS + HR, PCOLS), :] = zrows
    spat[pl.ds(0, FP), :] = jnp.zeros((FP, CH), BF16)
    spat[pl.ds(9 * FP, FP), :] = jnp.zeros((FP, CH), BF16)
    grad[15] = jnp.zeros((CHUNK, CH), F32)

    c_act.wait()
    x = actv[...].astype(F32).reshape(2 * FR, CH)
    ssum = jnp.sum(x, axis=0, keepdims=True)
    cen = x - ssum * (1.0 / (2 * FR))
    m2 = jnp.sum(cen * cen, axis=0, keepdims=True)
    r8 = lax.broadcasted_iota(jnp.int32, (8, CH), 0)
    stats[tm] = jnp.where(r8 == 0, ssum, jnp.where(r8 == 1, m2, 0.0))

    pl.semaphore_wait(barrier, len(peers))
    send("st_c", stats.at[tm], stats.at[tm], {"tm": tc})
    send("st_y", stats.at[tm], stats.at[tm], {"tm": ty})
    send("st_yc", stats.at[tm], stats.at[tm], {"tm": tyc})

    gi = lax.broadcasted_iota(jnp.int32, (CH, CH), 0)
    gj = lax.broadcasted_iota(jnp.int32, (CH, CH), 1)
    same = (((gi * 1639) >> 16) == ((gj * 1639) >> 16)).astype(F32)

    c_cot.wait()
    zpad = jnp.zeros((FP - FR, CH), F32)
    for i in range(2):
        cf = cotv[0, i].astype(F32).reshape(FR, CH)
        cotp[pl.ds(pl.multiple_of((2 * tm + i) * FP, FP), FP), :] = jnp.concatenate(
            [cf, zpad], axis=0
        ).astype(BF16)

    arrived("st_c", stats.at[tc], {"tm": tc})
    arrived("st_y", stats.at[ty], {"tm": ty})
    arrived("st_yc", stats.at[tyc], {"tm": tyc})
    st = [stats[i] for i in range(4)]
    total = st[0] + st[1] + st[2] + st[3]
    hi = lax.Precision.HIGHEST
    avg = dot(total, same, precision=hi)[0:1] * (1.0 / (8 * FR * GROUP))
    m2all = total[1:2]
    for i in range(4):
        dm = st[i][0:1] * (1.0 / (2 * FR)) - avg
        m2all = m2all + (2.0 * FR) * dm * dm
    m2all = jnp.broadcast_to(m2all, (8, CH))
    var = dot(m2all, same, precision=hi)[0:1] * (1.0 / (8 * FR * GROUP))
    inv = lax.rsqrt(var + EPS) * gain[...]
    bia = bias[...]

    for i in range(2):
        xf = actv[0, i].astype(F32).reshape(FR, CH)
        nf = (xf - avg) * inv + bia
        hf = nf * (1.0 / (1.0 + jnp.exp(-nf)))
        hf = jnp.concatenate(
            [hf.reshape(ROWS, COLS, CH), jnp.zeros((ROWS, PCOLS - COLS, CH), F32)], axis=1
        )
        hid[2 * tm + i, pl.ds(PCOLS, HR), :] = hf.reshape(HR, CH).astype(BF16)
        own = hid.at[2 * tm + i, pl.ds(PCOLS, HR), :]
        send(f"hy{i}", own, own, {"tm": ty})
        send(f"hc{i}", own, own, {"tm": tc})

    def cframes(t):
        return cotp.at[pl.ds(pl.multiple_of(2 * t * FP, FP), 2 * FP), :]

    send("cy", cframes(tm), cframes(tm), {"tm": ty})
    send("cc", cframes(tm), cframes(tm), {"tm": tc})

    def hframe(f):
        return hid.at[f, pl.ds(PCOLS, HR), :]

    def relay_hidden(i):
        return rc(f"hr{i}", hframe(2 * ty + i), hframe(2 * ty + i), {"tm": tc})

    def conv(f):
        acc = []
        for b in range(3):
            v = dot(hid[f, pl.ds(0, HR), :], wsv[b])
            for a in (1, 2):
                v = v + dot(hid[f, pl.ds(PCOLS * a, HR), :], wsv[3 * a + b])
            acc.append(v)
        o = acc[1] + pltpu.roll(acc[0], 1, 0) + pltpu.roll(acc[2], HR - 1, 0)
        o = o.reshape(ROWS, PCOLS, CH)[:, :COLS, :].reshape(FR, CH)
        return jnp.concatenate([o, zpad], axis=0)

    def sframe(f):
        return pl.ds(pl.multiple_of((f + 1) * FP, FP), FP)

    top, low = pl.ds(0, CUT), pl.ds(CUT, FP - CUT)

    def half_sums(h, base, extra):
        def step(j, _):
            q, r = lax.div(j, 2), lax.rem(j, 2)
            off = 2 + q - r - 2 * q * r
            val = conv(base + lax.rem(mp + off, 4))

            @pl.when(j == 0)
            def _():
                part[h, 0] = val.astype(BF16)
                rc(f"fr{h}", part.at[h, 0, top], far_r.at[h], xdev(1)).start()
                rc(f"fl{h}", part.at[h, 0, low], far_l.at[h], xdev(-1)).start()

            @pl.when(j == 1)
            def _():
                arrived(f"fr{h}", far_r.at[h], xdev(-1))
                up = val[:CUT] + far_r[h].astype(F32)
                part[h, 1, top] = up.astype(BF16)
                part[h, 1, low] = val[CUT:].astype(BF16)
                rc(f"nr{h}", part.at[h, 1], near.at[h, 0], xdev(1)).start()

            @pl.when(j == 2)
            def _():
                arrived(f"fl{h}", far_l.at[h], xdev(1))
                dn = val[CUT:] + far_l[h].astype(F32)
                part[h, 2, top] = val[:CUT].astype(BF16)
                part[h, 2, low] = dn.astype(BF16)
                rc(f"nl{h}", part.at[h, 2], near.at[h, 1], xdev(-1)).start()

            @pl.when(j == 3)
            def _():
                extra()
                arrived(f"nr{h}", near.at[h, 0], xdev(-1))
                arrived(f"nl{h}", near.at[h, 1], xdev(1))
                whole = val + near[h, 0].astype(F32) + near[h, 1].astype(F32)
                spat[sframe(base + mp), :] = whole.astype(BF16)

            return 0

        lax.fori_loop(0, 4, step, 0)
        started.append(rc(f"fr{h}", part.at[h, 0, top], far_r.at[h], xdev(1)))
        started.append(rc(f"fl{h}", part.at[h, 0, low], far_l.at[h], xdev(-1)))
        started.append(rc(f"nr{h}", part.at[h, 1], near.at[h, 0], xdev(1)))
        started.append(rc(f"nl{h}", part.at[h, 2], near.at[h, 1], xdev(-1)))
        mine = spat.at[sframe(base + mp), :]
        send(f"gr{h}", mine, mine, xdev(1))
        send(f"gl{h}", mine, mine, xdev(-1))

    def spart(f, lo, n):
        return spat.at[pl.ds(pl.multiple_of((f + 1) * FP + lo, 16), n), :]

    def forwards(h, base):
        lf, rf = base + lax.rem(mp + 3, 4), base + lax.rem(mp + 1, 4)
        return (
            rc(f"wr{h}", spart(lf, 0, CUT), spart(lf, 0, CUT), xdev(1)),
            rc(f"wl{h}", spart(rf, CUT, FP - CUT), spart(rf, CUT, FP - CUT), xdev(-1)),
        )

    def half_forward(h, base):
        lf, rf = base + lax.rem(mp + 3, 4), base + lax.rem(mp + 1, 4)
        to_r, to_l = forwards(h, base)
        arrived(f"gr{h}", spat.at[sframe(lf), :], xdev(-1))
        to_r.start()
        arrived(f"gl{h}", spat.at[sframe(rf), :], xdev(1))
        to_l.start()

    def half_done(h, base):
        ff = base + lax.rem(mp + 2, 4)
        arrived(f"wr{h}", spart(ff, 0, CUT), xdev(-1))
        arrived(f"wl{h}", spart(ff, CUT, FP - CUT), xdev(1))

    base0, base1 = 4 * yl, 4 * (1 - yl)
    c_ws.wait()
    for i in range(2):
        arrived(f"hc{i}", hframe(2 * tc + i), {"tm": tc})

    def relay_both():
        for i in range(2):
            arrived(f"hy{i}", hframe(2 * ty + i), {"tm": ty})
            relay_hidden(i).start()

    half_sums(0, base0, relay_both)
    for i in range(2):
        started.append(relay_hidden(i))
        arrived(f"hr{i}", hframe(2 * tyc + i), {"tm": tc})

    def between():
        half_forward(0, base0)

    half_sums(1, base1, between)
    arrived("cc", cframes(tc), {"tm": tc})
    arrived("cy", cframes(ty), {"tm": ty})
    send("cr", cframes(ty), cframes(ty), {"tm": tc})
    half_forward(1, base1)
    started.extend(forwards(0, base0))
    started.extend(forwards(1, base1))
    arrived("cr", cframes(tyc), {"tm": tc})
    half_done(0, base0)
    half_done(1, base1)
    c_wt.wait()

    for k in range(3):
        g = lax.dot_general(
            spat[pl.ds(k * FP, 8 * FP), :], cotp[...], (((0,), (0,)), ((), ())),
            preferred_element_type=F32,
        )
        grad[pl.ds(5 * k, 5)] = g.reshape(5, CHUNK, CH)

    def own(s):
        return grad[lax.rem(z + (s + 16), 16)]

    s2r[0] = own(8).astype(BF16)
    send("zr0", s2r.at[0], r2r.at[0], zdev(2))
    for i in (3, 2, 1, 0):
        s1r[i] = own(2 * i + 1).astype(BF16)
        send(f"or{i}", s1r.at[i], r1r.at[i], zdev(1))
        s1l[i] = own(-2 * i - 1).astype(BF16)
        send(f"ol{i}", s1l.at[i], r1l.at[i], zdev(-1))

    def temporal(t):
        r0 = pl.multiple_of(2 * t * FP, FP)
        v = dot(spat[pl.ds(r0, 2 * FP), :], wtv[0])
        for k in (1, 2):
            v = v + dot(spat[pl.ds(pl.multiple_of(r0 + k * FP, FP), 2 * FP), :], wtv[k])
        return v

    tsend0[...] = temporal(tyc)
    send("tp", tsend0, tpre, {"tm": tc})

    def chain_r(i):
        arrived(f"or{4 - i}", r1r.at[4 - i], zdev(-1))
        arrived(f"zr{i - 1}", r2r.at[i - 1], zdev(-2))
        v = own(8 - 2 * i) + r1r[4 - i].astype(F32) + r2r[i - 1].astype(F32)
        if i < 4:
            s2r[i] = v.astype(BF16)
            send(f"zr{i}", s2r.at[i], r2r.at[i], zdev(2))
        return v

    def chain_l(i):
        arrived(f"ol{3 - i}", r1l.at[3 - i], zdev(1))
        v = r1l[3 - i].astype(F32)
        if i > 0:
            arrived(f"zl{i - 1}", r2l.at[i - 1], zdev(2))
            v = v + r2l[i - 1].astype(F32)
        if i < 3:
            s2l[i] = (own(-6 + 2 * i) + v).astype(BF16)
            send(f"zl{i}", s2l.at[i], r2l.at[i], zdev(-2))
        return v

    chain_l(0)
    chain_r(1)
    tsend1[...] = temporal(tc)
    send("ts", tsend1, tsame, {"tm": tc})
    chain_l(1)
    chain_r(2)
    tacc = temporal(ty)
    arrived("tp", tpre, {"tm": tc})
    ysend[...] = (tacc + tpre[...]).astype(BF16)
    send("ty", ysend, yrecv, {"tm": ty})
    chain_l(2)
    chain_r(3)
    tsend_own = temporal(tm)
    arrived("ts", tsame, {"tm": tc})
    tsame[...] = tsame[...] + tsend_own
    yhs[...] = chain_l(3) + chain_r(4)
    send("yh", yhs, yhr, yhd)
    arrived("yh", yhr, yhd)
    gath[z] = ((yhs[...] + yhr[...]) * (1.0 / 32.0)).astype(BF16)

    def slot(s):
        return gath.at[lax.rem(z + (s + 32), 16)]

    send("ar0", slot(0), slot(0), zdev(2))
    send("al0", slot(0), slot(0), zdev(-2))
    send("br0", slot(0), slot(0), zdev(1))
    send("bl0", slot(0), slot(0), zdev(-1))
    arrived("ty", yrecv, {"tm": ty})
    res = tsame[...] + yrecv[...].astype(F32)
    for i in range(2):
        out[0, i] = res[i * FP : i * FP + FR].reshape(ROWS, COLS, CH).astype(BF16)
    for i in (1, 2, 3):
        arrived(f"ar{i - 1}", slot(-2 * i), zdev(-2))
        send(f"ar{i}", slot(-2 * i), slot(-2 * i), zdev(2))
        arrived(f"al{i - 1}", slot(2 * i), zdev(2))
        if i < 3:
            send(f"al{i}", slot(2 * i), slot(2 * i), zdev(-2))
        send(f"br{i}", slot(-2 * i), slot(-2 * i), zdev(1))
        send(f"bl{i}", slot(2 * i), slot(2 * i), zdev(-1))
    arrived("ar3", slot(-8), zdev(-2))
    for i in range(4):
        arrived(f"br{i}", slot(-2 * i - 1), zdev(-1))
        arrived(f"bl{i}", slot(2 * i + 1), zdev(1))
    for i in range(15):
        gout[pl.ds(i * CHUNK, CHUNK), :] = gath[i].astype(F32)
    for c in started:
        c.wait_send()


def body(activations, norm_gain, norm_bias, spatial_weight, temporal_weight, cotangent):
    anyspec = pl.BlockSpec(memory_space=pl.ANY)
    vm = pl.BlockSpec(memory_space=pltpu.VMEM)
    V = pltpu.VMEM
    zc = (CHUNK, CH)
    scratch = [
        V((1, 2, ROWS, COLS, CH), BF16),
        V((1, 2, ROWS, COLS, CH), BF16),
        V((9, CH, CH), BF16),
        V((3, CH, CH), BF16),
        V((4, 8, CH), F32),
        V((8, HR + 2 * PCOLS, CH), BF16),
        V((8 * FP, CH), BF16),
        V((2, 3, FP, CH), BF16),
        V((2, CUT, CH), BF16),
        V((2, FP - CUT, CH), BF16),
        V((2, 2, FP, CH), BF16),
        V((10 * FP, CH), BF16),
        V((16,) + zc, F32),
        V((4,) + zc, BF16),
        V((4,) + zc, BF16),
        V((4,) + zc, BF16),
        V((3,) + zc, BF16),
        V((4,) + zc, BF16),
        V((4,) + zc, BF16),
        V((4,) + zc, BF16),
        V((3,) + zc, BF16),
        V(zc, F32),
        V(zc, F32),
        V((16,) + zc, BF16),
        V((2 * FP, CH), F32),
        V((2 * FP, CH), F32),
        V((2 * FP, CH), F32),
        V((2 * FP, CH), F32),
        V((2 * FP, CH), BF16),
        V((2 * FP, CH), BF16),
        pltpu.SemaphoreType.DMA((4,)),
        pltpu.SemaphoreType.DMA((80,)),
        pltpu.SemaphoreType.DMA((80,)),
    ]
    out, gout = pl.pallas_call(
        kernel,
        out_shape=(
            jax.ShapeDtypeStruct((1, 2, ROWS, COLS, CH), BF16),
            jax.ShapeDtypeStruct((3 * CH, CH), F32),
        ),
        in_specs=[anyspec, vm, vm, anyspec, anyspec, anyspec],
        out_specs=(vm, vm),
        scratch_shapes=scratch,
        compiler_params=pltpu.CompilerParams(
            collective_id=0, has_side_effects=True, vmem_limit_bytes=48 * 2**20
        ),
        name="block",
    )(
        activations,
        norm_gain.reshape(1, CH),
        norm_bias.reshape(1, CH),
        spatial_weight,
        temporal_weight,
        cotangent,
    )
    return out, gout.reshape(3, CH, CH)


def solution(mesh):
    in_specs = (
        P("dp", "tm", None, None, "mp"),
        P("mp"),
        P("mp"),
        P(None, "mp", "tm"),
        P(None, "tm", "mp"),
        P("dp", "tm", None, None, "mp"),
    )
    out_specs = (P("dp", "tm", None, None, "mp"), P(None, "tm", "mp"))
    return jax.shard_map(body, mesh=mesh, in_specs=in_specs, out_specs=out_specs, check_vma=False)
```

time: 459 us -> 108 us (0.24)
  the two profiles are of different devices: /device:TPU:4 before, /device:TPU:2 now
where the time goes in v1:
time: 108 us
  Pallas kernels  99 us (92%)
  local copies, waits for them, and re-layouts  7.87 us (7%)
    pallas_call x1, Pallas kernels, body(): pl.pallas_call(kernel, out_shape=(jax.ShapeDtypeStruct((1, 2, ROWS, COLS,...  99 us
    unnamed x10, local copies, waits for them, and re-layouts  6.5 us

profile of v1, /device:TPU:2, one launch (start us, length us, event | category | flops | bytes accessed | tf_op | source)
XLA Modules:
  0.0 107.5 jit_solution(2688010140661612206)
XLA Ops:
  0.6 0.7 reshape.13.gain
  1.3 0.7 reshape.14.bias
  2.0 0.0 copy-start
  2.0 1.6 %copy-done = bf16[9,320,320]{2,1,0:T(8,128)(2,1)S(1)} copy-done((bf16[9,320,320]{2,1,0:T(8,128)(2,1)S(1)}, bf16[9,320,320]{2,1,0:T(8,128)(2,1)}, u32[]{:S(2)}) %copy-start) | copy-done | bytes 1843224
  3.6 0.0 copy-start.1
  3.6 1.1 %copy-done.1 = bf16[3,320,320]{2,1,0:T(8,128)(2,1)S(1)} copy-done((bf16[3,320,320]{2,1,0:T(8,128)(2,1)S(1)}, bf16[3,320,320]{2,1,0:T(8,128)(2,1)}, u32[]{:S(2)}) %copy-start.1) | copy-done | bytes 614424
  4.7 0.0 copy-start.2
  4.7 1.0 copy-done.2
  5.7 0.0 copy-start.3
  5.7 1.0 copy-done.3
  6.7 99.0 %block.1 = (bf16[1,2,5,40,320]{4,3,2,1,0:T(8,128)(2,1)S(1)}, f32[960,320]{1,0:T(8,128)S(1)}) custom-call(bf16[1,2,5,40,320]{4,3,2,1,0:T(8,128)(2,1)S(1)} %copy-done.2, f32[1,320]{1,0:T(1,128)S(1)} %reshape.13.gain, f32[1,320]{1,0:T(1,128)S(1)} %reshape.14.bias, bf16[9,320,320]{2,1,0:T(8,128)(2,1)S(1)} %copy-done, bf16[3,320,320]{2,1,0:T(8,128)(2,1)S(1)} %copy-done.1, ...), custom_call_target="tpu_custom_call" | custom-call | tf_op jit(solution)/shard_map/block/pallas_call | solution.py:402
  105.7 0.7 copy.10
  106.4 1.1 %copy.11 = f32[3,320,320]{2,1,0:T(8,128)} copy(f32[3,320,320]{2,1,0:T(8,128)S(1)} %bitcast.1) | data formatting | bytes 2457600
Async XLA Ops:
  2.0 1.6 %copy-start = (bf16[9,320,320]{2,1,0:T(8,128)(2,1)S(1)}, bf16[9,320,320]{2,1,0:T(8,128)(2,1)}, u32[]{:S(2)}) copy-start(bf16[9,320,320]{2,1,0:T(8,128)(2,1)} %ws.1) | copy-start | bytes 5529604
  3.6 1.1 %copy-start.1 = (bf16[3,320,320]{2,1,0:T(8,128)(2,1)S(1)}, bf16[3,320,320]{2,1,0:T(8,128)(2,1)}, u32[]{:S(2)}) copy-start(bf16[3,320,320]{2,1,0:T(8,128)(2,1)} %wt.1) | copy-start | bytes 1843204
  4.7 1.0 copy-start.2
  5.7 1.0 copy-start.3

commit v2 on v1

--- a/solution.py
+++ b/solution.py
@@ -15,7 +15,7 @@
 FP = 208
 CUT = 112
 HR = ROWS * PCOLS
-CHUNK = 64
+ZR = 160
 EPS = 1e-05
 
 
@@ -25,8 +25,8 @@
 
 def kernel(
     act, gain, bias, ws, wt, cot, out, gout,
-    actv, cotv, wsv, wtv, stats, hid, cotp, part, far_r, far_l, near, spat,
-    grad, s1r, s2r, s1l, s2l, r1r, r2r, r1l, r2l, yhs, yhr, gath,
+    actv, cotv, wsv, wtv, gainv, biasv, stats, hid, cotp, part, far_r, far_l, near, spat,
+    grad, s1r, s2r, s1l, s2l, r1r, r2r, r1l, r2l, yhs, yhr, gath, hold, mine,
     tpre, tsame, tsend0, tsend1, ysend, yrecv, lsem, ssem, rsem,
 ):
     dp, tm, mp = lax.axis_index("dp"), lax.axis_index("tm"), lax.axis_index("mp")
@@ -65,7 +65,9 @@
     c_ws = pltpu.make_async_copy(ws, wsv, lsem.at[1])
     c_cot = pltpu.make_async_copy(cot, cotv, lsem.at[2])
     c_wt = pltpu.make_async_copy(wt, wtv, lsem.at[3])
-    for c in (c_act, c_ws, c_cot, c_wt):
+    c_gain = pltpu.make_async_copy(gain, gainv, lsem.at[4])
+    c_bias = pltpu.make_async_copy(bias, biasv, lsem.at[5])
+    for c in (c_act, c_gain, c_bias, c_cot, c_ws, c_wt):
         c.start()
     yhd = {"dp": dp + 1 - 2 * yh}
     peers = [{"tm": tc}, {"tm": ty}, {"tm": tyc}, xdev(1), xdev(-1)]
@@ -79,7 +81,7 @@
     hid[:, pl.ds(PCOLS + HR, PCOLS), :] = zrows
     spat[pl.ds(0, FP), :] = jnp.zeros((FP, CH), BF16)
     spat[pl.ds(9 * FP, FP), :] = jnp.zeros((FP, CH), BF16)
-    grad[15] = jnp.zeros((CHUNK, CH), F32)
+    grad[15] = jnp.zeros((ZR, 128), F32)
 
     c_act.wait()
     x = actv[...].astype(F32).reshape(2 * FR, CH)
@@ -119,8 +121,10 @@
         m2all = m2all + (2.0 * FR) * dm * dm
     m2all = jnp.broadcast_to(m2all, (8, CH))
     var = dot(m2all, same, precision=hi)[0:1] * (1.0 / (8 * FR * GROUP))
-    inv = lax.rsqrt(var + EPS) * gain[...]
-    bia = bias[...]
+    c_gain.wait()
+    c_bias.wait()
+    inv = lax.rsqrt(var + EPS) * gainv[...].reshape(1, CH)
+    bia = biasv[...].reshape(1, CH)
 
     for i in range(2):
         xf = actv[0, i].astype(F32).reshape(FR, CH)
@@ -136,9 +140,6 @@
 
     def cframes(t):
         return cotp.at[pl.ds(pl.multiple_of(2 * t * FP, FP), 2 * FP), :]
-
-    send("cy", cframes(tm), cframes(tm), {"tm": ty})
-    send("cc", cframes(tm), cframes(tm), {"tm": tc})
 
     def hframe(f):
         return hid.at[f, pl.ds(PCOLS, HR), :]
@@ -162,52 +163,75 @@
 
     top, low = pl.ds(0, CUT), pl.ds(CUT, FP - CUT)
 
-    def half_sums(h, base, extra):
+    def far(h):
+        return (
+            rc(f"fr{h}", part.at[h, 0, top], far_r.at[h], xdev(1)),
+            rc(f"fl{h}", part.at[h, 0, low], far_l.at[h], xdev(-1)),
+        )
+
+    def near_early(h):
+        return (
+            rc(f"nrl{h}", part.at[h, 1, low], near.at[h, 0, low], xdev(1)),
+            rc(f"nlt{h}", part.at[h, 2, top], near.at[h, 1, top], xdev(-1)),
+        )
+
+    def gathers(h, base):
+        f = base + mp
+        t, b = spart(f, 0, CUT), spart(f, CUT, FP - CUT)
+        return (
+            rc(f"grt{h}", t, t, xdev(1)),
+            rc(f"glb{h}", b, b, xdev(-1)),
+            rc(f"grb{h}", b, b, xdev(1)),
+            rc(f"glt{h}", t, t, xdev(-1)),
+        )
+
+    def half_convs(h, base, hook):
         def step(j, _):
             q, r = lax.div(j, 2), lax.rem(j, 2)
             off = 2 + q - r - 2 * q * r
-            val = conv(base + lax.rem(mp + off, 4))
+            hold[j] = conv(base + lax.rem(mp + off, 4))
 
             @pl.when(j == 0)
             def _():
-                part[h, 0] = val.astype(BF16)
-                rc(f"fr{h}", part.at[h, 0, top], far_r.at[h], xdev(1)).start()
-                rc(f"fl{h}", part.at[h, 0, low], far_l.at[h], xdev(-1)).start()
+                part[h, 0] = hold[0].astype(BF16)
+                for c in far(h):
+                    c.start()
 
             @pl.when(j == 1)
             def _():
-                arrived(f"fr{h}", far_r.at[h], xdev(-1))
-                up = val[:CUT] + far_r[h].astype(F32)
-                part[h, 1, top] = up.astype(BF16)
-                part[h, 1, low] = val[CUT:].astype(BF16)
-                rc(f"nr{h}", part.at[h, 1], near.at[h, 0], xdev(1)).start()
+                part[h, 1, low] = hold[1, low].astype(BF16)
+                near_early(h)[0].start()
 
             @pl.when(j == 2)
             def _():
-                arrived(f"fl{h}", far_l.at[h], xdev(1))
-                dn = val[CUT:] + far_l[h].astype(F32)
-                part[h, 2, top] = val[:CUT].astype(BF16)
-                part[h, 2, low] = dn.astype(BF16)
-                rc(f"nl{h}", part.at[h, 2], near.at[h, 1], xdev(-1)).start()
-
-            @pl.when(j == 3)
-            def _():
-                extra()
-                arrived(f"nr{h}", near.at[h, 0], xdev(-1))
-                arrived(f"nl{h}", near.at[h, 1], xdev(1))
-                whole = val + near[h, 0].astype(F32) + near[h, 1].astype(F32)
-                spat[sframe(base + mp), :] = whole.astype(BF16)
-
+                part[h, 2, top] = hold[2, top].astype(BF16)
+                near_early(h)[1].start()
+
+            hook(j)
             return 0
 
         lax.fori_loop(0, 4, step, 0)
-        started.append(rc(f"fr{h}", part.at[h, 0, top], far_r.at[h], xdev(1)))
-        started.append(rc(f"fl{h}", part.at[h, 0, low], far_l.at[h], xdev(-1)))
-        started.append(rc(f"nr{h}", part.at[h, 1], near.at[h, 0], xdev(1)))
-        started.append(rc(f"nl{h}", part.at[h, 2], near.at[h, 1], xdev(-1)))
-        mine = spat.at[sframe(base + mp), :]
-        send(f"gr{h}", mine, mine, xdev(1))
-        send(f"gl{h}", mine, mine, xdev(-1))
+        started.extend(far(h))
+        started.extend(near_early(h))
+
+    def half_near(h):
+        arrived(f"fr{h}", far_r.at[h], xdev(-1))
+        part[h, 1, top] = (hold[1, top] + far_r[h].astype(F32)).astype(BF16)
+        send(f"nrt{h}", part.at[h, 1, top], near.at[h, 0, top], xdev(1))
+        arrived(f"fl{h}", far_l.at[h], xdev(1))
+        part[h, 2, low] = (hold[2, low] + far_l[h].astype(F32)).astype(BF16)
+        send(f"nll{h}", part.at[h, 2, low], near.at[h, 1, low], xdev(-1))
+        mine[...] = hold[3]
+
+    def half_sum(h, base):
+        arrived(f"nrl{h}", near.at[h, 0, low], xdev(-1))
+        arrived(f"nlt{h}", near.at[h, 1, top], xdev(1))
+        arrived(f"nrt{h}", near.at[h, 0, top], xdev(-1))
+        arrived(f"nll{h}", near.at[h, 1, low], xdev(1))
+        whole = mine[...] + near[h, 0].astype(F32) + near[h, 1].astype(F32)
+        spat[sframe(base + mp), :] = whole.astype(BF16)
+        for c in gathers(h, base):
+            c.start()
 
     def spart(f, lo, n):
         return spat.at[pl.ds(pl.multiple_of((f + 1) * FP + lo, 16), n), :]
@@ -222,13 +246,16 @@
     def half_forward(h, base):
         lf, rf = base + lax.rem(mp + 3, 4), base + lax.rem(mp + 1, 4)
         to_r, to_l = forwards(h, base)
-        arrived(f"gr{h}", spat.at[sframe(lf), :], xdev(-1))
+        arrived(f"grt{h}", spart(lf, 0, CUT), xdev(-1))
         to_r.start()
-        arrived(f"gl{h}", spat.at[sframe(rf), :], xdev(1))
+        arrived(f"glb{h}", spart(rf, CUT, FP - CUT), xdev(1))
         to_l.start()
 
     def half_done(h, base):
+        lf, rf = base + lax.rem(mp + 3, 4), base + lax.rem(mp + 1, 4)
         ff = base + lax.rem(mp + 2, 4)
+        arrived(f"grb{h}", spart(lf, CUT, FP - CUT), xdev(-1))
+        arrived(f"glt{h}", spart(rf, 0, CUT), xdev(1))
         arrived(f"wr{h}", spart(ff, 0, CUT), xdev(-1))
         arrived(f"wl{h}", spart(ff, CUT, FP - CUT), xdev(1))
 
@@ -237,48 +264,64 @@
     for i in range(2):
         arrived(f"hc{i}", hframe(2 * tc + i), {"tm": tc})
 
-    def relay_both():
-        for i in range(2):
-            arrived(f"hy{i}", hframe(2 * ty + i), {"tm": ty})
-            relay_hidden(i).start()
-
-    half_sums(0, base0, relay_both)
-    for i in range(2):
-        started.append(relay_hidden(i))
+    half_convs(0, base0, lambda j: None)
+    half_near(0)
+    for i in range(2):
+        arrived(f"hy{i}", hframe(2 * ty + i), {"tm": ty})
+        c = relay_hidden(i)
+        c.start()
+        started.append(c)
+    send("cy", cframes(tm), cframes(tm), {"tm": ty})
+    for i in range(2):
         arrived(f"hr{i}", hframe(2 * tyc + i), {"tm": tc})
 
-    def between():
-        half_forward(0, base0)
-
-    half_sums(1, base1, between)
+    def between(j):
+        @pl.when(j == 1)
+        def _():
+            half_sum(0, base0)
+
+    half_convs(1, base1, between)
+    started.extend(gathers(0, base0))
+    half_near(1)
+    send("cc", cframes(tm), cframes(tm), {"tm": tc})
+    half_forward(0, base0)
+    started.extend(forwards(0, base0))
+    half_sum(1, base1)
+    started.extend(gathers(1, base1))
     arrived("cc", cframes(tc), {"tm": tc})
     arrived("cy", cframes(ty), {"tm": ty})
     send("cr", cframes(ty), cframes(ty), {"tm": tc})
     half_forward(1, base1)
-    started.extend(forwards(0, base0))
     started.extend(forwards(1, base1))
     arrived("cr", cframes(tyc), {"tm": tc})
     half_done(0, base0)
     half_done(1, base1)
     c_wt.wait()
 
+    tails = []
     for k in range(3):
         g = lax.dot_general(
             spat[pl.ds(k * FP, 8 * FP), :], cotp[...], (((0,), (0,)), ((), ())),
             preferred_element_type=F32,
         )
-        grad[pl.ds(5 * k, 5)] = g.reshape(5, CHUNK, CH)
+        for a in range(2):
+            grad[pl.ds(4 * k + 2 * a, 2)] = g[:, 128 * a : 128 * a + 128].reshape(2, ZR, 128)
+        tails.append(g[:, 256:])
+    grad[pl.ds(12, 2)] = jnp.concatenate(tails[:2], axis=1).reshape(2, ZR, 128)
+    grad[14] = jnp.concatenate([tails[2][:ZR], tails[2][ZR:]], axis=1)
 
     def own(s):
         return grad[lax.rem(z + (s + 16), 16)]
 
+    def one_hop(i):
+        s1r[i] = own(2 * i + 1).astype(BF16)
+        s1l[i] = own(-2 * i - 1).astype(BF16)
+        send(f"or{i}", s1r.at[i], r1r.at[i], zdev(1))
+        send(f"ol{i}", s1l.at[i], r1l.at[i], zdev(-1))
+
     s2r[0] = own(8).astype(BF16)
     send("zr0", s2r.at[0], r2r.at[0], zdev(2))
-    for i in (3, 2, 1, 0):
-        s1r[i] = own(2 * i + 1).astype(BF16)
-        send(f"or{i}", s1r.at[i], r1r.at[i], zdev(1))
-        s1l[i] = own(-2 * i - 1).astype(BF16)
-        send(f"ol{i}", s1l.at[i], r1l.at[i], zdev(-1))
+    one_hop(3)
 
     def temporal(t):
         r0 = pl.multiple_of(2 * t * FP, FP)
@@ -312,16 +355,19 @@
 
     chain_l(0)
     chain_r(1)
+    one_hop(2)
     tsend1[...] = temporal(tc)
     send("ts", tsend1, tsame, {"tm": tc})
     chain_l(1)
     chain_r(2)
+    one_hop(1)
     tacc = temporal(ty)
     arrived("tp", tpre, {"tm": tc})
     ysend[...] = (tacc + tpre[...]).astype(BF16)
     send("ty", ysend, yrecv, {"tm": ty})
     chain_l(2)
     chain_r(3)
+    one_hop(0)
     tsend_own = temporal(tm)
     arrived("ts", tsame, {"tm": tc})
     tsame[...] = tsame[...] + tsend_own
@@ -349,26 +395,36 @@
             send(f"al{i}", slot(2 * i), slot(2 * i), zdev(-2))
         send(f"br{i}", slot(-2 * i), slot(-2 * i), zdev(1))
         send(f"bl{i}", slot(2 * i), slot(2 * i), zdev(-1))
-    arrived("ar3", slot(-8), zdev(-2))
     for i in range(4):
         arrived(f"br{i}", slot(-2 * i - 1), zdev(-1))
         arrived(f"bl{i}", slot(2 * i + 1), zdev(1))
-    for i in range(15):
-        gout[pl.ds(i * CHUNK, CHUNK), :] = gath[i].astype(F32)
+    arrived("ar3", slot(-8), zdev(-2))
+    for j in range(12):
+        k, a, b = j // 4, j // 2 % 2, j % 2
+        gout[k, pl.ds(b * ZR, ZR), pl.ds(128 * a, 128)] = gath[j].astype(F32)
+    for b in range(2):
+        v = gath[12 + b].astype(F32)
+        gout[0, pl.ds(b * ZR, ZR), pl.ds(256, 64)] = v[:, :64]
+        gout[1, pl.ds(b * ZR, ZR), pl.ds(256, 64)] = v[:, 64:]
+    v = gath[14].astype(F32)
+    gout[2, pl.ds(0, ZR), pl.ds(256, 64)] = v[:, :64]
+    gout[2, pl.ds(ZR, ZR), pl.ds(256, 64)] = v[:, 64:]
     for c in started:
         c.wait_send()
 
 
 def body(activations, norm_gain, norm_bias, spatial_weight, temporal_weight, cotangent):
-    anyspec = pl.BlockSpec(memory_space=pl.ANY)
     vm = pl.BlockSpec(memory_space=pltpu.VMEM)
+    hbm = pl.BlockSpec(memory_space=pltpu.HBM)
     V = pltpu.VMEM
-    zc = (CHUNK, CH)
+    zc = (ZR, 128)
     scratch = [
         V((1, 2, ROWS, COLS, CH), BF16),
         V((1, 2, ROWS, COLS, CH), BF16),
         V((9, CH, CH), BF16),
         V((3, CH, CH), BF16),
+        V((CH,), F32),
+        V((CH,), F32),
         V((4, 8, CH), F32),
         V((8, HR + 2 * PCOLS, CH), BF16),
         V((8 * FP, CH), BF16),
@@ -389,38 +445,39 @@
         V(zc, F32),
         V(zc, F32),
         V((16,) + zc, BF16),
+        V((4, FP, CH), F32),
+        V((FP, CH), F32),
         V((2 * FP, CH), F32),
         V((2 * FP, CH), F32),
         V((2 * FP, CH), F32),
         V((2 * FP, CH), F32),
         V((2 * FP, CH), BF16),
         V((2 * FP, CH), BF16),
-        pltpu.SemaphoreType.DMA((4,)),
+        pltpu.SemaphoreType.DMA((6,)),
         pltpu.SemaphoreType.DMA((80,)),
         pltpu.SemaphoreType.DMA((80,)),
     ]
-    out, gout = pl.pallas_call(
+    return pl.pallas_call(
         kernel,
         out_shape=(
             jax.ShapeDtypeStruct((1, 2, ROWS, COLS, CH), BF16),
-            jax.ShapeDtypeStruct((3 * CH, CH), F32),
+            jax.ShapeDtypeStruct((3, CH, CH), F32),
         ),
-        in_specs=[anyspec, vm, vm, anyspec, anyspec, anyspec],
+        in_specs=[hbm] * 6,
         out_specs=(vm, vm),
         scratch_shapes=scratch,
         compiler_params=pltpu.CompilerParams(
-            collective_id=0, has_side_effects=True, vmem_limit_bytes=48 * 2**20
+            collective_id=0, has_side_effects=True, vmem_limit_bytes=60 * 2**20
         ),
         name="block",
     )(
         activations,
-        norm_gain.reshape(1, CH),
-        norm_bias.reshape(1, CH),
+        norm_gain,
+        norm_bias,
         spatial_weight,
         temporal_weight,
         cotangent,
     )
-    return out, gout.reshape(3, CH, CH)
 
 
 def solution(mesh):

time: 108 us -> 97.9 us (0.906)
  Pallas kernels: 99 us -> 92.8 us
  local copies, waits for them, and re-layouts: 7.87 us -> 4.29 us
    pallas_call x1, Pallas kernels: 99 us -> 92.8 us  [body(): pl.pallas_call(kernel, out_shape=(jax.ShapeDtypeStruct((1, 2, ROWS, COLS,...]
    unnamed x10 -> x2, local copies, waits for them, and re-layouts: 6.5 us -> 4.29 us
    reshape x2 -> x0, local copies, waits for them, and re-layouts: 1.37 us -> none  [the longest x1 0.68 us: body(): norm_gain.reshape(1, CH)]
where the time goes in v2:
time: 97.9 us; the launch traced here: 97.7 us
  Pallas kernels  92.8 us (95%)
  local copies, waits for them, and re-layouts  4.29 us (4%)
    pallas_call x1, Pallas kernels, body(): pl.pallas_call(kernel, out_shape=(jax.ShapeDtypeStruct((1, 2, ROWS, COLS,...  92.8 us
    unnamed x2, local copies, waits for them, and re-layouts  4.29 us

profile of v2, /device:TPU:2, one launch (start us, length us, event | category | flops | bytes accessed | tf_op | source)
XLA Modules:
  0.0 97.7 jit_solution(14919726821357160826)
XLA Ops:
  0.6 92.8 %block.1 = (bf16[1,2,5,40,320]{4,3,2,1,0:T(8,128)(2,1)}, f32[3,320,320]{2,1,0:T(8,128)}) custom-call(bf16[1,2,5,40,320]{4,3,2,1,0:T(8,128)(2,1)} %act.1, f32[320]{0:T(512)} %gain.1, f32[320]{0:T(512)} %bias.1, bf16[9,320,320]{2,1,0:T(8,128)(2,1)} %ws.1, bf16[3,320,320]{2,1,0:T(8,128)(2,1)} %wt.1, bf16[1,2,5,40,320]{4,3,2,1,0:T(8,128)(2,1)} %cot.1), custom_call_target="tpu_custom_call" | custom-call | tf_op jit(solution)/shard_map/block/pallas_call | solution.py:460
  93.4 1.7 %copy.10 = bf16[1,2,5,40,320]{4,3,2,1,0:T(8,128)(2,1)} copy(bf16[1,2,5,40,320]{4,3,2,1,0:T(8,128)(2,1)} %get-tuple-element.4) | data formatting | bytes 512000
  95.1 2.6 %copy.11 = f32[3,320,320]{2,1,0:T(8,128)} copy(f32[3,320,320]{2,1,0:T(8,128)} %get-tuple-element.5) | data formatting | bytes 2457600

commit v3 on v2

--- a/solution.py
+++ b/solution.py
@@ -16,6 +16,7 @@
 CUT = 112
 HR = ROWS * PCOLS
 ZR = 160
+HZ = ZR // 2
 EPS = 1e-05
 
 
@@ -310,8 +311,30 @@
     grad[pl.ds(12, 2)] = jnp.concatenate(tails[:2], axis=1).reshape(2, ZR, 128)
     grad[14] = jnp.concatenate([tails[2][:ZR], tails[2][ZR:]], axis=1)
 
+    order = (8, 7, -7, 6, -6, 5, -5, 4, -4, 3, -3, 2, -2, 1, -1, 0)
+    bounds = (0, 3, 7, 11, 15, 16)
+    mine_z = pl.ds(pl.multiple_of(yh * HZ, HZ), HZ)
+    other_z = pl.ds(pl.multiple_of((1 - yh) * HZ, HZ), HZ)
+
+    def at_z(s):
+        return lax.rem(z + (s + 32), 16)
+
+    def group(g):
+        return pl.ds(bounds[g], bounds[g + 1] - bounds[g])
+
+    for g in range(5):
+        for p in range(bounds[g], bounds[g + 1]):
+            yhs[p] = grad[at_z(order[p]), other_z, :].astype(BF16)
+        send(f"yg{g}", yhs.at[group(g)], yhr.at[group(g)], yhd)
+    got = set()
+
     def own(s):
-        return grad[lax.rem(z + (s + 16), 16)]
+        p = order.index(s)
+        g = max(i for i in range(5) if bounds[i] <= p)
+        if g not in got:
+            got.add(g)
+            arrived(f"yg{g}", yhr.at[group(g)], yhd)
+        return grad[at_z(s), mine_z, :] + yhr[p].astype(F32)
 
     def one_hop(i):
         s1r[i] = own(2 * i + 1).astype(BF16)
@@ -371,18 +394,19 @@
     tsend_own = temporal(tm)
     arrived("ts", tsame, {"tm": tc})
     tsame[...] = tsame[...] + tsend_own
-    yhs[...] = chain_l(3) + chain_r(4)
-    send("yh", yhs, yhr, yhd)
-    arrived("yh", yhr, yhd)
-    gath[z] = ((yhs[...] + yhr[...]) * (1.0 / 32.0)).astype(BF16)
+    gath[z, mine_z, :] = ((chain_l(3) + chain_r(4)) * (1.0 / 32.0)).astype(BF16)
 
     def slot(s):
-        return gath.at[lax.rem(z + (s + 32), 16)]
+        return gath.at[at_z(s), mine_z, :]
+
+    def hand(s):
+        send(f"yf{s}", slot(s), slot(s), yhd)
 
     send("ar0", slot(0), slot(0), zdev(2))
     send("al0", slot(0), slot(0), zdev(-2))
     send("br0", slot(0), slot(0), zdev(1))
     send("bl0", slot(0), slot(0), zdev(-1))
+    hand(0)
     arrived("ty", yrecv, {"tm": ty})
     res = tsame[...] + yrecv[...].astype(F32)
     for i in range(2):
@@ -395,10 +419,20 @@
             send(f"al{i}", slot(2 * i), slot(2 * i), zdev(-2))
         send(f"br{i}", slot(-2 * i), slot(-2 * i), zdev(1))
         send(f"bl{i}", slot(2 * i), slot(2 * i), zdev(-1))
-    for i in range(4):
-        arrived(f"br{i}", slot(-2 * i - 1), zdev(-1))
-        arrived(f"bl{i}", slot(2 * i + 1), zdev(1))
+        hand(-2 * i)
+        hand(2 * i)
+        arrived(f"br{i - 1}", slot(1 - 2 * i), zdev(-1))
+        hand(1 - 2 * i)
+        arrived(f"bl{i - 1}", slot(2 * i - 1), zdev(1))
+        hand(2 * i - 1)
     arrived("ar3", slot(-8), zdev(-2))
+    hand(-8)
+    arrived("br3", slot(-7), zdev(-1))
+    hand(-7)
+    arrived("bl3", slot(7), zdev(1))
+    hand(7)
+    for s in (0, -2, 2, -1, 1, -4, 4, -3, 3, -6, 6, -5, 5, -8, -7, 7):
+        arrived(f"yf{s}", gath.at[at_z(s), other_z, :], yhd)
     for j in range(12):
         k, a, b = j // 4, j // 2 % 2, j % 2
         gout[k, pl.ds(b * ZR, ZR), pl.ds(128 * a, 128)] = gath[j].astype(F32)
@@ -417,7 +451,7 @@
     vm = pl.BlockSpec(memory_space=pltpu.VMEM)
     hbm = pl.BlockSpec(memory_space=pltpu.HBM)
     V = pltpu.VMEM
-    zc = (ZR, 128)
+    zc = (HZ, 128)
     scratch = [
         V((1, 2, ROWS, COLS, CH), BF16),
         V((1, 2, ROWS, COLS, CH), BF16),
@@ -433,7 +467,7 @@
         V((2, FP - CUT, CH), BF16),
         V((2, 2, FP, CH), BF16),
         V((10 * FP, CH), BF16),
-        V((16,) + zc, F32),
+        V((16, ZR, 128), F32),
         V((4,) + zc, BF16),
         V((4,) + zc, BF16),
         V((4,) + zc, BF16),
@@ -442,9 +476,9 @@
         V((4,) + zc, BF16),
         V((4,) + zc, BF16),
         V((3,) + zc, BF16),
-        V(zc, F32),
-        V(zc, F32),
         V((16,) + zc, BF16),
+        V((16,) + zc, BF16),
+        V((16, ZR, 128), BF16),
         V((4, FP, CH), F32),
         V((FP, CH), F32),
         V((2 * FP, CH), F32),
@@ -454,8 +488,8 @@
         V((2 * FP, CH), BF16),
         V((2 * FP, CH), BF16),
         pltpu.SemaphoreType.DMA((6,)),
-        pltpu.SemaphoreType.DMA((80,)),
-        pltpu.SemaphoreType.DMA((80,)),
+        pltpu.SemaphoreType.DMA((112,)),
+        pltpu.SemaphoreType.DMA((112,)),
     ]
     return pl.pallas_call(
         kernel,
@@ -467,16 +501,16 @@
         out_specs=(vm, vm),
         scratch_shapes=scratch,
         compiler_params=pltpu.CompilerParams(
-            collective_id=0, has_side_effects=True, vmem_limit_bytes=60 * 2**20
+            collective_id=0, has_side_effects=True, vmem_limit_bytes=48 * 2**20
         ),
         name="block",
     )(
-        activations,
-        norm_gain,
-        norm_bias,
-        spatial_weight,
-        temporal_weight,
-        cotangent,
+        *(
+            pltpu.with_memory_space_constraint(v, pltpu.HBM)
+            for v in (
+                activations, norm_gain, norm_bias, spatial_weight, temporal_weight, cotangent,
+            )
+        )
     )
 
 

time: 97.9 us -> 93.2 us (0.952)
  the two profiles are of different devices: /device:TPU:2 before, /device:TPU:8 now
where the time goes in v3:
time: 93.2 us; the launch traced here: 93.1 us
  Pallas kernels  90.6 us (97%)
  local copies, waits for them, and re-layouts  1.83 us (2%)
    pallas_call x1, Pallas kernels, body(): pl.pallas_call(kernel, out_shape=(jax.ShapeDtypeStruct((1, 2, ROWS, COLS,...  90.6 us

profile of v3, /device:TPU:8, one launch (start us, length us, event | category | flops | bytes accessed | tf_op | source)
XLA Modules:
  0.0 93.1 jit_solution(8160046800665115970)
XLA Ops:
  0.6 90.6 %block.1 = (bf16[1,2,5,40,320]{4,3,2,1,0:T(8,128)(2,1)S(1)}, f32[3,320,320]{2,1,0:T(8,128)S(1)}) custom-call(bf16[1,2,5,40,320]{4,3,2,1,0:T(8,128)(2,1)} %act.1, f32[320]{0:T(512)} %gain.1, f32[320]{0:T(512)} %bias.1, bf16[9,320,320]{2,1,0:T(8,128)(2,1)} %ws.1, bf16[3,320,320]{2,1,0:T(8,128)(2,1)} %wt.1, bf16[1,2,5,40,320]{4,3,2,1,0:T(8,128)(2,1)} %cot.1), custom_call_target="tpu_custom_call" | custom-call | tf_op jit(solution)/shard_map/block/pallas_call | solution.py:494
  91.2 0.7 copy.10
  92.0 1.1 %copy.11 = f32[3,320,320]{2,1,0:T(8,128)} copy(f32[3,320,320]{2,1,0:T(8,128)S(1)} %get-tuple-element.5) | data formatting | bytes 2457600

commit v4 on v3

--- a/solution.py
+++ b/solution.py
@@ -27,7 +27,7 @@
 def kernel(
     act, gain, bias, ws, wt, cot, out, gout,
     actv, cotv, wsv, wtv, gainv, biasv, stats, hid, cotp, part, far_r, far_l, near, spat,
-    grad, s1r, s2r, s1l, s2l, r1r, r2r, r1l, r2l, yhs, yhr, gath, hold, mine,
+    grad, sr, sl, rr, rl, yhs, yhr, gath, hold, mine,
     tpre, tsame, tsend0, tsend1, ysend, yrecv, lsem, ssem, rsem,
 ):
     dp, tm, mp = lax.axis_index("dp"), lax.axis_index("tm"), lax.axis_index("mp")
@@ -72,7 +72,7 @@
         c.start()
     yhd = {"dp": dp + 1 - 2 * yh}
     peers = [{"tm": tc}, {"tm": ty}, {"tm": tyc}, xdev(1), xdev(-1)]
-    peers += [zdev(1), zdev(-1), zdev(2), zdev(-2), yhd]
+    peers += [zdev(h) for h in (1, 2, 3, 4, -1, -2, -3, -4)] + [yhd]
     barrier = pltpu.get_barrier_semaphore()
     for p in peers:
         pl.semaphore_signal(barrier, inc=1, device_id=p, device_id_type=MESH)
@@ -322,10 +322,13 @@
     def group(g):
         return pl.ds(bounds[g], bounds[g + 1] - bounds[g])
 
-    for g in range(5):
+    def send_group(g):
         for p in range(bounds[g], bounds[g + 1]):
             yhs[p] = grad[at_z(order[p]), other_z, :].astype(BF16)
         send(f"yg{g}", yhs.at[group(g)], yhr.at[group(g)], yhd)
+
+    send_group(0)
+    send_group(1)
     got = set()
 
     def own(s):
@@ -334,17 +337,29 @@
         if g not in got:
             got.add(g)
             arrived(f"yg{g}", yhr.at[group(g)], yhd)
+            if g < 3:
+                send_group(g + 2)
         return grad[at_z(s), mine_z, :] + yhr[p].astype(F32)
 
-    def one_hop(i):
-        s1r[i] = own(2 * i + 1).astype(BF16)
-        s1l[i] = own(-2 * i - 1).astype(BF16)
-        send(f"or{i}", s1r.at[i], r1r.at[i], zdev(1))
-        send(f"ol{i}", s1l.at[i], r1l.at[i], zdev(-1))
-
-    s2r[0] = own(8).astype(BF16)
-    send("zr0", s2r.at[0], r2r.at[0], zdev(2))
-    one_hop(3)
+    ways = ((1, sr, rr), (-1, sl, rl))
+
+    def hops(i):
+        return i - 4 if i > 4 else i
+
+    def terms(*far_to_near):
+        for i in far_to_near:
+            for d, snd, rcv in ways[: 1 if i == 8 else 2]:
+                snd[i - 1] = own(d * i).astype(BF16)
+                send(f"z{d}_{i}", snd.at[i - 1], rcv.at[i - 1], zdev(d * hops(i)))
+
+    def incoming(d, rcv, steps):
+        v = None
+        for i in steps:
+            if d * i != -8:
+                arrived(f"z{d}_{i}", rcv.at[i - 1], zdev(-d * hops(i)))
+                t = rcv[i - 1].astype(F32)
+                v = t if v is None else v + t
+        return v
 
     def temporal(t):
         r0 = pl.multiple_of(2 * t * FP, FP)
@@ -355,46 +370,24 @@
 
     tsend0[...] = temporal(tyc)
     send("tp", tsend0, tpre, {"tm": tc})
-
-    def chain_r(i):
-        arrived(f"or{4 - i}", r1r.at[4 - i], zdev(-1))
-        arrived(f"zr{i - 1}", r2r.at[i - 1], zdev(-2))
-        v = own(8 - 2 * i) + r1r[4 - i].astype(F32) + r2r[i - 1].astype(F32)
-        if i < 4:
-            s2r[i] = v.astype(BF16)
-            send(f"zr{i}", s2r.at[i], r2r.at[i], zdev(2))
-        return v
-
-    def chain_l(i):
-        arrived(f"ol{3 - i}", r1l.at[3 - i], zdev(1))
-        v = r1l[3 - i].astype(F32)
-        if i > 0:
-            arrived(f"zl{i - 1}", r2l.at[i - 1], zdev(2))
-            v = v + r2l[i - 1].astype(F32)
-        if i < 3:
-            s2l[i] = (own(-6 + 2 * i) + v).astype(BF16)
-            send(f"zl{i}", s2l.at[i], r2l.at[i], zdev(-2))
-        return v
-
-    chain_l(0)
-    chain_r(1)
-    one_hop(2)
+    terms(8, 7, 6, 5)
     tsend1[...] = temporal(tc)
     send("ts", tsend1, tsame, {"tm": tc})
-    chain_l(1)
-    chain_r(2)
-    one_hop(1)
+    terms(3, 2, 1)
+    for d, snd, rcv in ways:
+        snd[3] = (own(4 * d) + incoming(d, rcv, (5, 6, 7, 8))).astype(BF16)
+        send(f"z{d}_4", snd.at[3], rcv.at[3], zdev(4 * d))
     tacc = temporal(ty)
     arrived("tp", tpre, {"tm": tc})
     ysend[...] = (tacc + tpre[...]).astype(BF16)
     send("ty", ysend, yrecv, {"tm": ty})
-    chain_l(2)
-    chain_r(3)
-    one_hop(0)
     tsend_own = temporal(tm)
     arrived("ts", tsame, {"tm": tc})
     tsame[...] = tsame[...] + tsend_own
-    gath[z, mine_z, :] = ((chain_l(3) + chain_r(4)) * (1.0 / 32.0)).astype(BF16)
+    zsum = own(0)
+    for d, snd, rcv in ways:
+        zsum = zsum + incoming(d, rcv, (1, 2, 3, 4))
+    gath[z, mine_z, :] = (zsum * (1.0 / 32.0)).astype(BF16)
 
     def slot(s):
         return gath.at[at_z(s), mine_z, :]
@@ -402,36 +395,31 @@
     def hand(s):
         send(f"yf{s}", slot(s), slot(s), yhd)
 
-    send("ar0", slot(0), slot(0), zdev(2))
-    send("al0", slot(0), slot(0), zdev(-2))
-    send("br0", slot(0), slot(0), zdev(1))
-    send("bl0", slot(0), slot(0), zdev(-1))
+    for h in (4, 3, 2, 1):
+        for d in (1, -1):
+            send(f"a{d}_{h}", slot(0), slot(0), zdev(d * h))
     hand(0)
+    for h in (1, 2, 3):
+        for d in (1, -1):
+            arrived(f"a{d}_{h}", slot(-d * h), zdev(-d * h))
+            hand(-d * h)
+    for d in (1, -1):
+        arrived(f"a{d}_4", slot(-4 * d), zdev(-4 * d))
+        for h in (4, 3, 2, 1):
+            if d * h != -4:
+                send(f"b{d}_{h}", slot(-4 * d), slot(-4 * d), zdev(d * h))
+    for d in (1, -1):
+        hand(-4 * d)
     arrived("ty", yrecv, {"tm": ty})
     res = tsame[...] + yrecv[...].astype(F32)
     for i in range(2):
         out[0, i] = res[i * FP : i * FP + FR].reshape(ROWS, COLS, CH).astype(BF16)
-    for i in (1, 2, 3):
-        arrived(f"ar{i - 1}", slot(-2 * i), zdev(-2))
-        send(f"ar{i}", slot(-2 * i), slot(-2 * i), zdev(2))
-        arrived(f"al{i - 1}", slot(2 * i), zdev(2))
-        if i < 3:
-            send(f"al{i}", slot(2 * i), slot(2 * i), zdev(-2))
-        send(f"br{i}", slot(-2 * i), slot(-2 * i), zdev(1))
-        send(f"bl{i}", slot(2 * i), slot(2 * i), zdev(-1))
-        hand(-2 * i)
-        hand(2 * i)
-        arrived(f"br{i - 1}", slot(1 - 2 * i), zdev(-1))
-        hand(1 - 2 * i)
-        arrived(f"bl{i - 1}", slot(2 * i - 1), zdev(1))
-        hand(2 * i - 1)
-    arrived("ar3", slot(-8), zdev(-2))
-    hand(-8)
-    arrived("br3", slot(-7), zdev(-1))
-    hand(-7)
-    arrived("bl3", slot(7), zdev(1))
-    hand(7)
-    for s in (0, -2, 2, -1, 1, -4, 4, -3, 3, -6, 6, -5, 5, -8, -7, 7):
+    for h in (1, 2, 3, 4):
+        for d in (1, -1):
+            if d * h != -4:
+                arrived(f"b{d}_{h}", slot(-d * (h + 4)), zdev(-d * h))
+                hand(-d * (h + 4))
+    for s in range(-8, 8):
         arrived(f"yf{s}", gath.at[at_z(s), other_z, :], yhd)
     for j in range(12):
         k, a, b = j // 4, j // 2 % 2, j % 2
@@ -468,14 +456,10 @@
         V((2, 2, FP, CH), BF16),
         V((10 * FP, CH), BF16),
         V((16, ZR, 128), F32),
-        V((4,) + zc, BF16),
-        V((4,) + zc, BF16),
-        V((4,) + zc, BF16),
-        V((3,) + zc, BF16),
-        V((4,) + zc, BF16),
-        V((4,) + zc, BF16),
-        V((4,) + zc, BF16),
-        V((3,) + zc, BF16),
+        V((8,) + zc, BF16),
+        V((8,) + zc, BF16),
+        V((8,) + zc, BF16),
+        V((8,) + zc, BF16),
         V((16,) + zc, BF16),
         V((16,) + zc, BF16),
         V((16, ZR, 128), BF16),

time: 93.2 us -> 89.6 us (0.961)
  the two profiles are of different devices: /device:TPU:8 before, /device:TPU:4 now
where the time goes in v4:
time: 89.6 us; the launch traced here: 89.5 us
  Pallas kernels  87 us (97%)
  local copies, waits for them, and re-layouts  1.83 us (2%)
    pallas_call x1, Pallas kernels, body(): pl.pallas_call(kernel, out_shape=(jax.ShapeDtypeStruct((1, 2, ROWS, COLS,...  87 us
    unnamed x2, local copies, waits for them, and re-layouts  1.83 us

profile of v4, /device:TPU:4, one launch (start us, length us, event | category | flops | bytes accessed | tf_op | source)
XLA Modules:
  0.0 89.5 jit_solution(10638943393553305782)
XLA Ops:
  0.6 87.0 %block.1 = (bf16[1,2,5,40,320]{4,3,2,1,0:T(8,128)(2,1)S(1)}, f32[3,320,320]{2,1,0:T(8,128)S(1)}) custom-call(bf16[1,2,5,40,320]{4,3,2,1,0:T(8,128)(2,1)} %act.1, f32[320]{0:T(512)} %gain.1, f32[320]{0:T(512)} %bias.1, bf16[9,320,320]{2,1,0:T(8,128)(2,1)} %ws.1, bf16[3,320,320]{2,1,0:T(8,128)(2,1)} %wt.1, bf16[1,2,5,40,320]{4,3,2,1,0:T(8,128)(2,1)} %cot.1), custom_call_target="tpu_custom_call" | custom-call | tf_op jit(solution)/shard_map/block/pallas_call | solution.py:478
  87.6 0.7 copy.10
  88.3 1.1 %copy.11 = f32[3,320,320]{2,1,0:T(8,128)} copy(f32[3,320,320]{2,1,0:T(8,128)S(1)} %get-tuple-element.5) | data formatting | bytes 2457600

commit v5 on v4

--- a/solution.py
+++ b/solution.py
@@ -13,7 +13,8 @@
 ROWS, COLS, PCOLS = 5, 40, 48
 FR = ROWS * COLS
 FP = 208
-CUT = 112
+DT, DL = 240, 288
+DR = DT + DL
 HR = ROWS * PCOLS
 ZR = 160
 HZ = ZR // 2
@@ -27,7 +28,7 @@
 def kernel(
     act, gain, bias, ws, wt, cot, out, gout,
     actv, cotv, wsv, wtv, gainv, biasv, stats, hid, cotp, part, far_r, far_l, near, spat,
-    grad, sr, sl, rr, rl, yhs, yhr, gath, hold, mine,
+    grad, sr, sl, rr, rl, yhs, yhr, gath, hold, mine, dsp, gacc,
     tpre, tsame, tsend0, tsend1, ysend, yrecv, lsem, ssem, rsem,
 ):
     dp, tm, mp = lax.axis_index("dp"), lax.axis_index("tm"), lax.axis_index("mp")
@@ -80,8 +81,9 @@
     zrows = jnp.zeros((8, PCOLS, CH), BF16)
     hid[:, pl.ds(0, PCOLS), :] = zrows
     hid[:, pl.ds(PCOLS + HR, PCOLS), :] = zrows
-    spat[pl.ds(0, FP), :] = jnp.zeros((FP, CH), BF16)
-    spat[pl.ds(9 * FP, FP), :] = jnp.zeros((FP, CH), BF16)
+    for end in (0, 9):
+        spat[pl.ds(end * FP, FP), :] = jnp.zeros((FP, CH), BF16)
+        cotp[pl.ds(end * FP, FP), :] = jnp.zeros((FP, CH), BF16)
     grad[15] = jnp.zeros((ZR, 128), F32)
 
     c_act.wait()
@@ -105,7 +107,7 @@
     zpad = jnp.zeros((FP - FR, CH), F32)
     for i in range(2):
         cf = cotv[0, i].astype(F32).reshape(FR, CH)
-        cotp[pl.ds(pl.multiple_of((2 * tm + i) * FP, FP), FP), :] = jnp.concatenate(
+        cotp[pl.ds(pl.multiple_of((2 * tm + i + 1) * FP, FP), FP), :] = jnp.concatenate(
             [cf, zpad], axis=0
         ).astype(BF16)
 
@@ -140,7 +142,7 @@
         send(f"hc{i}", own, own, {"tm": tc})
 
     def cframes(t):
-        return cotp.at[pl.ds(pl.multiple_of(2 * t * FP, FP), 2 * FP), :]
+        return cotp.at[pl.ds(pl.multiple_of((2 * t + 1) * FP, FP), 2 * FP), :]
 
     def hframe(f):
         return hid.at[f, pl.ds(PCOLS, HR), :]
@@ -159,10 +161,39 @@
         o = o.reshape(ROWS, PCOLS, CH)[:, :COLS, :].reshape(FR, CH)
         return jnp.concatenate([o, zpad], axis=0)
 
-    def sframe(f):
-        return pl.ds(pl.multiple_of((f + 1) * FP, FP), FP)
-
-    top, low = pl.ds(0, CUT), pl.ds(CUT, FP - CUT)
+    top, low = pl.ds(0, DT), pl.ds(DT, DL)
+
+    def pack(j, v):
+        t = v[:, 256:]
+        hold[j, pl.ds(0, 96)] = v[:96, :128]
+        hold[j, pl.ds(96, 96)] = v[:96, 128:256]
+        hold[j, pl.ds(192, 48)] = jnp.concatenate([t[:48], t[48:96]], axis=1)
+        hold[j, pl.ds(240, 112)] = v[96:, :128]
+        hold[j, pl.ds(352, 112)] = v[96:, 128:256]
+        last = jnp.concatenate([t[160:], jnp.zeros((16, 64), F32)], axis=0)
+        hold[j, pl.ds(464, 64)] = jnp.concatenate([t[96:160], last], axis=1)
+
+    def unpack(base):
+        def step(i, _):
+            f = base + i
+            r = (f + 1) * FP
+
+            def put(lo, n, lane, width, v):
+                spat[pl.ds(pl.multiple_of(r + lo, 16), n), pl.ds(lane, width)] = v
+
+            put(0, 96, 0, 128, dsp[f, pl.ds(0, 96)])
+            put(0, 96, 128, 128, dsp[f, pl.ds(96, 96)])
+            t = dsp[f, pl.ds(192, 48)].astype(F32)
+            put(0, 48, 256, 64, t[:, :64].astype(BF16))
+            put(48, 48, 256, 64, t[:, 64:].astype(BF16))
+            put(96, 112, 0, 128, dsp[f, pl.ds(240, 112)])
+            put(96, 112, 128, 128, dsp[f, pl.ds(352, 112)])
+            t = dsp[f, pl.ds(464, 64)].astype(F32)
+            put(96, 64, 256, 64, t[:, :64].astype(BF16))
+            put(160, 48, 256, 64, t[:48, 64:].astype(BF16))
+            return 0
+
+        lax.fori_loop(0, 4, step, 0)
 
     def far(h):
         return (
@@ -178,7 +209,7 @@
 
     def gathers(h, base):
         f = base + mp
-        t, b = spart(f, 0, CUT), spart(f, CUT, FP - CUT)
+        t, b = dsp.at[f, top], dsp.at[f, low]
         return (
             rc(f"grt{h}", t, t, xdev(1)),
             rc(f"glb{h}", b, b, xdev(-1)),
@@ -190,7 +221,7 @@
         def step(j, _):
             q, r = lax.div(j, 2), lax.rem(j, 2)
             off = 2 + q - r - 2 * q * r
-            hold[j] = conv(base + lax.rem(mp + off, 4))
+            pack(j, conv(base + lax.rem(mp + off, 4)))
 
             @pl.when(j == 0)
             def _():
@@ -230,35 +261,32 @@
         arrived(f"nrt{h}", near.at[h, 0, top], xdev(-1))
         arrived(f"nll{h}", near.at[h, 1, low], xdev(1))
         whole = mine[...] + near[h, 0].astype(F32) + near[h, 1].astype(F32)
-        spat[sframe(base + mp), :] = whole.astype(BF16)
+        dsp[base + mp] = whole.astype(BF16)
         for c in gathers(h, base):
             c.start()
-
-    def spart(f, lo, n):
-        return spat.at[pl.ds(pl.multiple_of((f + 1) * FP + lo, 16), n), :]
 
     def forwards(h, base):
         lf, rf = base + lax.rem(mp + 3, 4), base + lax.rem(mp + 1, 4)
         return (
-            rc(f"wr{h}", spart(lf, 0, CUT), spart(lf, 0, CUT), xdev(1)),
-            rc(f"wl{h}", spart(rf, CUT, FP - CUT), spart(rf, CUT, FP - CUT), xdev(-1)),
+            rc(f"wr{h}", dsp.at[lf, top], dsp.at[lf, top], xdev(1)),
+            rc(f"wl{h}", dsp.at[rf, low], dsp.at[rf, low], xdev(-1)),
         )
 
     def half_forward(h, base):
         lf, rf = base + lax.rem(mp + 3, 4), base + lax.rem(mp + 1, 4)
         to_r, to_l = forwards(h, base)
-        arrived(f"grt{h}", spart(lf, 0, CUT), xdev(-1))
+        arrived(f"grt{h}", dsp.at[lf, top], xdev(-1))
         to_r.start()
-        arrived(f"glb{h}", spart(rf, CUT, FP - CUT), xdev(1))
+        arrived(f"glb{h}", dsp.at[rf, low], xdev(1))
         to_l.start()
 
     def half_done(h, base):
         lf, rf = base + lax.rem(mp + 3, 4), base + lax.rem(mp + 1, 4)
         ff = base + lax.rem(mp + 2, 4)
-        arrived(f"grb{h}", spart(lf, CUT, FP - CUT), xdev(-1))
-        arrived(f"glt{h}", spart(rf, 0, CUT), xdev(1))
-        arrived(f"wr{h}", spart(ff, 0, CUT), xdev(-1))
-        arrived(f"wl{h}", spart(ff, CUT, FP - CUT), xdev(1))
+        arrived(f"grb{h}", dsp.at[lf, low], xdev(-1))
+        arrived(f"glt{h}", dsp.at[rf, top], xdev(1))
+        arrived(f"wr{h}", dsp.at[ff, top], xdev(-1))
+        arrived(f"wl{h}", dsp.at[ff, low], xdev(1))
 
     base0, base1 = 4 * yl, 4 * (1 - yl)
     c_ws.wait()
@@ -292,19 +320,28 @@
     arrived("cc", cframes(tc), {"tm": tc})
     arrived("cy", cframes(ty), {"tm": ty})
     send("cr", cframes(ty), cframes(ty), {"tm": tc})
+    half_done(0, base0)
+    unpack(base0)
     half_forward(1, base1)
     started.extend(forwards(1, base1))
     arrived("cr", cframes(tyc), {"tm": tc})
-    half_done(0, base0)
+    def half_grad(k, base):
+        return lax.dot_general(
+            spat[pl.ds(pl.multiple_of((base + 1) * FP, FP), 4 * FP), :],
+            cotp[pl.ds(pl.multiple_of((base + 2 - k) * FP, FP), 4 * FP), :],
+            (((0,), (0,)), ((), ())),
+            preferred_element_type=F32,
+        )
+
+    for k in range(3):
+        gacc[k] = half_grad(k, base0)
     half_done(1, base1)
+    unpack(base1)
     c_wt.wait()
 
     tails = []
     for k in range(3):
-        g = lax.dot_general(
-            spat[pl.ds(k * FP, 8 * FP), :], cotp[...], (((0,), (0,)), ((), ())),
-            preferred_element_type=F32,
-        )
+        g = gacc[k] + half_grad(k, base1)
         for a in range(2):
             grad[pl.ds(4 * k + 2 * a, 2)] = g[:, 128 * a : 128 * a + 128].reshape(2, ZR, 128)
         tails.append(g[:, 256:])
@@ -449,11 +486,11 @@
         V((CH,), F32),
         V((4, 8, CH), F32),
         V((8, HR + 2 * PCOLS, CH), BF16),
-        V((8 * FP, CH), BF16),
-        V((2, 3, FP, CH), BF16),
-        V((2, CUT, CH), BF16),
-        V((2, FP - CUT, CH), BF16),
-        V((2, 2, FP, CH), BF16),
+        V((10 * FP, CH), BF16),
+        V((2, 3, DR, 128), BF16),
+        V((2, DT, 128), BF16),
+        V((2, DL, 128), BF16),
+        V((2, 2, DR, 128), BF16),
         V((10 * FP, CH), BF16),
         V((16, ZR, 128), F32),
         V((8,) + zc, BF16),
@@ -463,8 +500,10 @@
         V((16,) + zc, BF16),
         V((16,) + zc, BF16),
         V((16, ZR, 128), BF16),
-        V((4, FP, CH), F32),
-        V((FP, CH), F32),
+        V((4, DR, 128), F32),
+        V((DR, 128), F32),
+        V((8, DR, 128), BF16),
+        V((3, CH, CH), F32),
         V((2 * FP, CH), F32),
         V((2 * FP, CH), F32),
         V((2 * FP, CH), F32),

time: 89.6 us -> 88.2 us (0.984)
  Pallas kernels: 87 us -> 85.6 us
    pallas_call x1, Pallas kernels: 87 us -> 85.6 us  [body(): pl.pallas_call(kernel, out_shape=(jax.ShapeDtypeStruct((1, 2, ROWS, COLS,...]
where the time goes in v5:
time: 88.2 us; the launch traced here: 88 us
  Pallas kernels  85.6 us (97%)
  local copies, waits for them, and re-layouts  1.83 us (2%)
    pallas_call x1, Pallas kernels, body(): pl.pallas_call(kernel, out_shape=(jax.ShapeDtypeStruct((1, 2, ROWS, COLS,...  85.6 us
    unnamed x2, local copies, waits for them, and re-layouts  1.83 us

profile of v5, /device:TPU:4, one launch (start us, length us, event | category | flops | bytes accessed | tf_op | source)
XLA Modules:
  0.0 88.0 jit_solution(12948483520402602290)
XLA Ops:
  0.6 85.6 %block.1 = (bf16[1,2,5,40,320]{4,3,2,1,0:T(8,128)(2,1)S(1)}, f32[3,320,320]{2,1,0:T(8,128)S(1)}) custom-call(bf16[1,2,5,40,320]{4,3,2,1,0:T(8,128)(2,1)} %act.1, f32[320]{0:T(512)} %gain.1, f32[320]{0:T(512)} %bias.1, bf16[9,320,320]{2,1,0:T(8,128)(2,1)} %ws.1, bf16[3,320,320]{2,1,0:T(8,128)(2,1)} %wt.1, bf16[1,2,5,40,320]{4,3,2,1,0:T(8,128)(2,1)} %cot.1), custom_call_target="tpu_custom_call" | custom-call | tf_op jit(solution)/shard_map/block/pallas_call | solution.py:517
  86.2 0.7 copy.10
  86.9 1.1 %copy.11 = f32[3,320,320]{2,1,0:T(8,128)} copy(f32[3,320,320]{2,1,0:T(8,128)S(1)} %get-tuple-element.5) | data formatting | bytes 2457600

commit v6 on v5

--- a/solution.py
+++ b/solution.py
@@ -69,7 +69,7 @@
     c_wt = pltpu.make_async_copy(wt, wtv, lsem.at[3])
     c_gain = pltpu.make_async_copy(gain, gainv, lsem.at[4])
     c_bias = pltpu.make_async_copy(bias, biasv, lsem.at[5])
-    for c in (c_act, c_gain, c_bias, c_cot, c_ws, c_wt):
+    for c in (c_act, c_gain, c_bias):
         c.start()
     yhd = {"dp": dp + 1 - 2 * yh}
     peers = [{"tm": tc}, {"tm": ty}, {"tm": tyc}, xdev(1), xdev(-1)]
@@ -87,6 +87,8 @@
     grad[15] = jnp.zeros((ZR, 128), F32)
 
     c_act.wait()
+    for c in (c_cot, c_ws, c_wt):
+        c.start()
     x = actv[...].astype(F32).reshape(2 * FR, CH)
     ssum = jnp.sum(x, axis=0, keepdims=True)
     cen = x - ssum * (1.0 / (2 * FR))
@@ -101,7 +103,15 @@
 
     gi = lax.broadcasted_iota(jnp.int32, (CH, CH), 0)
     gj = lax.broadcasted_iota(jnp.int32, (CH, CH), 1)
-    same = (((gi * 1639) >> 16) == ((gj * 1639) >> 16)).astype(F32)
+    same = (((gi * 1639) >> 16) == ((gj * 1639) >> 16)).astype(F32).astype(BF16)
+
+    def group_sums(v):
+        p1 = v.astype(BF16).astype(F32)
+        p2 = (v - p1).astype(BF16).astype(F32)
+        p3 = v - p1 - p2
+        parts = jnp.concatenate([p1, p2, p3, jnp.zeros_like(v)], axis=0)
+        o = dot(parts.astype(BF16), same)
+        return (o[0:8] + o[8:16] + o[16:24])[0:1]
 
     c_cot.wait()
     zpad = jnp.zeros((FP - FR, CH), F32)
@@ -116,14 +126,13 @@
     arrived("st_yc", stats.at[tyc], {"tm": tyc})
     st = [stats[i] for i in range(4)]
     total = st[0] + st[1] + st[2] + st[3]
-    hi = lax.Precision.HIGHEST
-    avg = dot(total, same, precision=hi)[0:1] * (1.0 / (8 * FR * GROUP))
+    avg = group_sums(total) * (1.0 / (8 * FR * GROUP))
     m2all = total[1:2]
     for i in range(4):
         dm = st[i][0:1] * (1.0 / (2 * FR)) - avg
         m2all = m2all + (2.0 * FR) * dm * dm
     m2all = jnp.broadcast_to(m2all, (8, CH))
-    var = dot(m2all, same, precision=hi)[0:1] * (1.0 / (8 * FR * GROUP))
+    var = group_sums(m2all) * (1.0 / (8 * FR * GROUP))
     c_gain.wait()
     c_bias.wait()
     inv = lax.rsqrt(var + EPS) * gainv[...].reshape(1, CH)
@@ -456,20 +465,26 @@
             if d * h != -4:
                 arrived(f"b{d}_{h}", slot(-d * (h + 4)), zdev(-d * h))
                 hand(-d * (h + 4))
+    for c in started:
+        c.wait_send()
+
+    def write(sel, off):
+        for j in range(12):
+            k, a, b = j // 4, j // 2 % 2, j % 2
+            rows = pl.ds(pl.multiple_of(off + b * ZR, 16), HZ)
+            gout[k, rows, pl.ds(128 * a, 128)] = gath[j, sel, :].astype(F32)
+        for b in range(2):
+            rows = pl.ds(pl.multiple_of(off + b * ZR, 16), HZ)
+            v = gath[12 + b, sel, :].astype(F32)
+            gout[0, rows, pl.ds(256, 64)] = v[:, :64]
+            gout[1, rows, pl.ds(256, 64)] = v[:, 64:]
+            v = gath[14, sel, :].astype(F32)
+            gout[2, rows, pl.ds(256, 64)] = v[:, 64 * b : 64 * b + 64]
+
+    write(mine_z, yh * HZ)
     for s in range(-8, 8):
         arrived(f"yf{s}", gath.at[at_z(s), other_z, :], yhd)
-    for j in range(12):
-        k, a, b = j // 4, j // 2 % 2, j % 2
-        gout[k, pl.ds(b * ZR, ZR), pl.ds(128 * a, 128)] = gath[j].astype(F32)
-    for b in range(2):
-        v = gath[12 + b].astype(F32)
-        gout[0, pl.ds(b * ZR, ZR), pl.ds(256, 64)] = v[:, :64]
-        gout[1, pl.ds(b * ZR, ZR), pl.ds(256, 64)] = v[:, 64:]
-    v = gath[14].astype(F32)
-    gout[2, pl.ds(0, ZR), pl.ds(256, 64)] = v[:, :64]
-    gout[2, pl.ds(ZR, ZR), pl.ds(256, 64)] = v[:, 64:]
-    for c in started:
-        c.wait_send()
+    write(other_z, (1 - yh) * HZ)
 
 
 def body(activations, norm_gain, norm_bias, spatial_weight, temporal_weight, cotangent):

time: 88.2 us -> 87.3 us (0.990)
  the two profiles are of different devices: /device:TPU:4 before, /device:TPU:32 now
where the time goes in v6:
time: 87.3 us; the launch traced here: 87.2 us
  Pallas kernels  84.7 us (97%)
  local copies, waits for them, and re-layouts  1.83 us (2%)
    pallas_call x1, Pallas kernels, body(): pl.pallas_call(kernel, out_shape=(jax.ShapeDtypeStruct((1, 2, ROWS, COLS,...  84.7 us
    unnamed x2, local copies, waits for them, and re-layouts  1.83 us

profile of v6, /device:TPU:32, one launch (start us, length us, event | category | flops | bytes accessed | tf_op | source)
XLA Modules:
  0.0 87.2 jit_solution(9277865004702078276)
XLA Ops:
  0.6 84.7 %block.1 = (bf16[1,2,5,40,320]{4,3,2,1,0:T(8,128)(2,1)S(1)}, f32[3,320,320]{2,1,0:T(8,128)S(1)}) custom-call(bf16[1,2,5,40,320]{4,3,2,1,0:T(8,128)(2,1)} %act.1, f32[320]{0:T(512)} %gain.1, f32[320]{0:T(512)} %bias.1, bf16[9,320,320]{2,1,0:T(8,128)(2,1)} %ws.1, bf16[3,320,320]{2,1,0:T(8,128)(2,1)} %wt.1, bf16[1,2,5,40,320]{4,3,2,1,0:T(8,128)(2,1)} %cot.1), custom_call_target="tpu_custom_call" | custom-call | tf_op jit(solution)/shard_map/block/pallas_call | solution.py:532
  85.4 0.7 copy.10
  86.1 1.1 %copy.11 = f32[3,320,320]{2,1,0:T(8,128)} copy(f32[3,320,320]{2,1,0:T(8,128)S(1)} %get-tuple-element.5) | data formatting | bytes 2457600
